TPU v7x, 32 devices: a whole 2x2x4 slice. The times are simulated.
32 devices in a mesh: seg: 8 (over z, core), cfg: 4 (over y, x).
Axes of the slice: x: 2, y: 2, z: 4, core: 2. Of those that a mesh axis runs over, the one named last changes fastest.
Arguments:
- node_feats: bfloat16 [128, 2048, 256], P('cfg', 'seg'), may hold values from -6 to 6
- adjacency: int32 [2048, 288], P('seg'), may hold values 0 or 1
- halo_rows: int32 [8, 2, 16], P('seg'), may hold values from 0 to 255
- node_graph: int32 [2048], P('seg'), may hold values from 0 to 3, never falling along the last dimension, each value on 1 to 1536 neighbouring positions
- layer_weights: bfloat16 [3, 256, 256], replicated, may hold values from -0.375 to 0.375
- bilinear: bfloat16 [256, 256], replicated, may hold values from -0.0234375 to 0.0234375
- partners: int32 [4, 128, 64], P(None, 'cfg'), may hold values from 0 to 127
- ranking: int32 [4, 128], replicated, may hold values from 0 to 127, each once within a row
Outputs:
- embeddings: bfloat16 [4, 128, 256], P(None, 'cfg')
- weight_grad: float32 [256, 256], replicated
- hinge_loss: float32 [], replicated
Inputs may be any that keep to these rules, and one draw needn't show every extreme that they name: `adjacency`: columns are, in order, the 16 rows read from the previous segment, the segment's own 256 nodes, the 16 rows read from the next segment. halo_rows[s, 0, :] are rows of segment s read by segment s-1, halo_rows[s, 1, :] rows read by segment s+1; repeats may occur. `node_graph`: never falls along the nodes; each graph has 1 to 1536 nodes, one exactly that many. `ranking`: each row is a permutation.
All inputs are finite; a program needn't handle non-finite values. No bound on the sum of `adjacency` on one device may be relied on, other than what follows from the above.
Results may differ from a plain program's by a relative error of at most 0.0034.
Values may be sent and summed in bfloat16 or wider, within the bound.
A program may use at most 64 MiB of HBM per device.

v0:
```python
import jax
import jax.numpy as jnp
from jax import lax
from jax.sharding import PartitionSpec as P

P_SIZE = 64
G = 4


high_precision_mode = lax.Precision.HIGHEST
eps = 1e-06


def with_halo(block, sides, width):
    for axis, dim in sides:
        count = lax.axis_size(axis)
        forward = [(i, i + 1) for i in range(count - 1)]
        backward = [(target, source) for source, target in forward]
        low = lax.ppermute(
            lax.slice_in_dim(block, block.shape[dim] - width, None, axis=dim), axis, forward
        )
        high = lax.ppermute(lax.slice_in_dim(block, 0, width, axis=dim), axis, backward)
        block = jnp.concatenate([low, block, high], axis=dim)
    return block


def rms_scale(values):
    return values * lax.rsqrt(jnp.mean(values * values, axis=-1, keepdims=True) + eps)


def conv_layer(hidden, adj_weights, degree, own_halo, weight, rim_rows):
    outgoing = jnp.concatenate(
        [jnp.take(hidden, own_halo[0], axis=1), jnp.take(hidden, own_halo[1], axis=1)], axis=1
    )
    framed = with_halo(outgoing, (("seg", 1),), rim_rows)
    extended = jnp.concatenate([framed[:, :rim_rows], hidden, framed[:, 3 * rim_rows :]], axis=1)
    summed = jnp.einsum("nm,cmf->cnf", adj_weights, extended, preferred_element_type=jnp.float32)
    mixed = (summed + hidden.astype(jnp.float32)) / (1.0 + degree)[None, :, None]
    normed = rms_scale(mixed).astype(jnp.bfloat16)
    branch = jnp.einsum("cnf,fg->cng", normed, weight, preferred_element_type=jnp.float32)
    return (hidden.astype(jnp.float32) + jax.nn.silu(branch)).astype(jnp.bfloat16)


def on_device(
    node_feats, adjacency, halo_rows, node_graph, layer_weights, bilinear, partners, ranking
):
    configs = node_feats.shape[0]
    feat_width = node_feats.shape[2]
    rim_rows = halo_rows.shape[2]
    adj_weights = adjacency.astype(jnp.bfloat16)
    degree = jnp.sum(adjacency, axis=1).astype(jnp.float32)
    hidden = node_feats
    for layer_idx in range(layer_weights.shape[0]):
        hidden = conv_layer(
            hidden, adj_weights, degree, halo_rows[0], layer_weights[layer_idx], rim_rows
        )
    onehot = (node_graph[None, :] == jnp.arange(G, dtype=jnp.int32)[:, None]).astype(jnp.bfloat16)
    pooled = jnp.einsum("gn,cnf->gcf", onehot, hidden, preferred_element_type=jnp.float32)
    flat_pooled = pooled.reshape(G * configs, feat_width)
    seg_count = lax.axis_size("seg")
    own_count = G * configs // seg_count
    seg_pos = lax.axis_index("seg")
    cfg_pos = lax.axis_index("cfg")
    seg_total = lax.psum_scatter(flat_pooled, "seg", scatter_dimension=0, tiled=True)
    own_emb = rms_scale(seg_total).astype(jnp.bfloat16)
    emb_flat = lax.all_gather(own_emb, "seg", axis=0, tiled=True)
    emb_cfg = emb_flat.reshape(G, configs, feat_width)
    everyone = lax.all_gather(emb_cfg, "cfg", axis=1, tiled=True)
    total_configs = everyone.shape[1]
    flat_index = seg_pos * own_count + jnp.arange(own_count, dtype=jnp.int32)
    row_graph = flat_index // configs
    global_config = cfg_pos * configs + flat_index % configs
    my_partners = lax.dynamic_slice_in_dim(
        partners.reshape(G * configs, -1), seg_pos * own_count, own_count, 0
    )
    graph_pick = (row_graph[:, None] == jnp.arange(G, dtype=jnp.int32)[None, :]).astype(jnp.float32)
    table = jnp.einsum(
        "rg,gqf->rqf", graph_pick, everyone.astype(jnp.float32), precision=high_precision_mode
    )
    rank_rows = jnp.einsum(
        "rg,gq->rq", graph_pick, ranking.astype(jnp.float32), precision=high_precision_mode
    )
    config_ids = jnp.arange(total_configs, dtype=jnp.int32)
    own_rank = jnp.sum(
        jnp.where(config_ids[None, :] == global_config[:, None], rank_rows, 0.0), axis=1
    )
    partner_hit = (my_partners[:, :, None] == config_ids[None, None, :]).astype(jnp.float32)
    projected_rows = jnp.dot(own_emb, bilinear, preferred_element_type=jnp.float32)
    all_scores = jnp.einsum("rh,rqh->rq", projected_rows, table, precision=high_precision_mode)
    config_scores = jnp.take_along_axis(all_scores, my_partners, axis=1)
    their_rank = jnp.take_along_axis(rank_rows, my_partners, axis=1)
    pairwise_direction = jnp.sign(their_rank - own_rank[:, None])
    margin = 1.0 - pairwise_direction * config_scores
    loss_part = jnp.sum(jax.nn.softplus(margin))
    pairwise_factor = -pairwise_direction * jax.nn.sigmoid(margin) / (G * P_SIZE)
    dense_coef = jnp.einsum(
        "rp,rpq->rq", pairwise_factor, partner_hit, precision=high_precision_mode
    )
    carry_over_rows = jnp.einsum("rq,rqh->rh", dense_coef, table, precision=high_precision_mode)
    grad_part = jnp.dot(
        own_emb.astype(jnp.float32).T, carry_over_rows, precision=high_precision_mode
    )
    weight_grad, loss_total = lax.psum((grad_part, loss_part), ("seg", "cfg"))
    return (emb_cfg, weight_grad, loss_total / (G * total_configs * P_SIZE))


def solution(mesh):
    placed = (
        P("cfg", "seg", None),
        P("seg", None),
        P("seg", None, None),
        P("seg"),
        P(),
        P(),
        P(None, "cfg", None),
        P(),
    )
    return jax.shard_map(
        on_device,
        mesh=mesh,
        in_specs=placed,
        out_specs=(P(None, "cfg", None), P(), P()),
        check_vma=False,
    )
```

profile of v0, /device:TPU:0, one launch (start us, length us, event | category | flops | bytes accessed | tf_op | source)
XLA Modules:
  0.0 325.5 jit_solution(11377313548413868607)
XLA Ops:
  7.2 0.8 compare_and_fusion.2
  8.0 2.0 gather_fusion
  10.0 0.1 select_bitcast_fusion.5
  10.1 2.4 collective-permute-start
  12.5 2.0 gather_fusion.1
  14.5 0.1 select_bitcast_fusion.4
  14.6 1.3 collective-permute-start.1
  15.9 6.4 %copy.56 = bf16[32,256,256]{1,2,0:T(8,128)(2,1)} copy(bf16[32,256,256]{2,1,0:T(8,128)(2,1)} %param.12) | data formatting | bytes 8388608 | tf_op args[0]
  22.4 5.8 %multiply_reduce_fusion.2 = (f32[32,256]{1,0:T(8,128)S(1)}, f32[32,256,256]{1,2,0:T(8,128)S(1)}) fusion(f32[256]{0:T(256)S(1)} %convert_add_fusion.6, bf16[32,256,256]{1,2,0:T(8,128)(2,1)} %copy.56, s32[256,288]{0,1:T(8,128)S(1)} %copy-done.3, bf16[32,16,256]{2,1,0:T(8,128)(2,1)S(1)} %collective-permute-done.1, bf16[32,256,256]{2,1,0:T(8,128)(2,1)} %param.12, ...), kind=kOutput, calls=%fused_computation.25 | convolution fusion | flops 1232666624 | bytes 17630208 | tf_op jit(solution)/shard_map/nm,cmf->cnf/dot_general | solution.py:37
  28.2 5.5 %fusion.1 = bf16[32,256,256]{1,2,0:T(8,128)(2,1)} fusion(bf16[32,256,256]{1,2,0:T(8,128)(2,1)S(1)} %copy-done.2, f32[32,256,256]{1,2,0:T(8,128)S(1)} %get-tuple-element.19, f32[32,256]{1,0:T(8,128)S(1)} %add_rsqrt_fusion.2, bf16[3,256,256]{2,1,0:T(8,128)(2,1)} %param.16), kind=kOutput, calls=%fused_computation.15 | convolution fusion | flops 1092616192 | bytes 16941056 | tf_op jit(solution)/shard_map/cnf,fg->cng/dot_general | solution.py:40
  33.7 7.9 %copy.60 = bf16[32,256,256]{2,0,1:T(8,128)(2,1)} copy(bf16[32,256,256]{1,2,0:T(8,128)(2,1)} %fusion.1) | data formatting | bytes 8388608 | tf_op jit(solution)/shard_map/convert_element_type | solution.py:41
  41.6 2.7 gather_fusion.2
  44.4 2.8 gather_fusion.3
  47.1 0.1 select_bitcast_fusion.3
  47.2 0.2 copy.61
  47.4 5.2 %collective-permute-start.2 = (bf16[32,16,256]{2,1,0:T(8,128)(2,1)S(1)}, bf16[32,16,256]{2,1,0:T(8,128)(2,1)S(1)}, u32[]{:S(2)}, u32[]{:S(2)}) collective-permute-start(bf16[32,16,256]{2,1,0:T(8,128)(2,1)S(1)} %copy.61), channel_id=1, source_target_pairs={{0,4},{4,8},{8,12},{12,16},{16,20},{20,24},{24,28},{1,5},{5,9},{9,... | collective-permute-start | bytes 786440 | tf_op jit(solution)/shard_map/ppermute | solution.py:19
  52.6 0.1 select_bitcast_fusion.2
  52.7 0.2 copy.63
  52.9 1.3 collective-permute-start.3
  54.2 1.0 copy.64
  55.2 2.3 collective-permute-done.3
  57.5 1.8 copy.65
  59.3 9.2 %multiply_reduce_fusion.1 = (f32[32,256]{1,0:T(8,128)S(1)}, f32[32,256,256]{1,2,0:T(8,128)S(1)}) fusion(f32[256]{0:T(256)S(1)} %convert_add_fusion.6, bf16[32,256,256]{1,2,0:T(8,128)(2,1)} %fusion.1, s32[256,288]{0,1:T(8,128)S(1)} %copy-done.3, bf16[32,16,256]{1,2,0:T(8,128)(2,1)} %copy.65, bf16[32,16,256]{1,2,0:T(8,128)(2,1)S(1)} %copy.64), kind=kOutput, calls=%fused_computation.23 | convolution fusion | flops 1232666624 | bytes 13435904 | tf_op jit(solution)/shard_map/nm,cmf->cnf/dot_general | solution.py:37
  68.5 5.5 %fusion.3 = bf16[32,256,256]{1,2,0:T(8,128)(2,1)} fusion(bf16[32,256,256]{1,2,0:T(8,128)(2,1)S(1)} %copy-done.1, f32[32,256,256]{1,2,0:T(8,128)S(1)} %get-tuple-element.21, f32[32,256]{1,0:T(8,128)S(1)} %add_rsqrt_fusion.1, bf16[3,256,256]{2,1,0:T(8,128)(2,1)} %param.16), kind=kOutput, calls=%fused_computation.17 | convolution fusion | flops 1092616192 | bytes 16941056 | tf_op jit(solution)/shard_map/cnf,fg->cng/dot_general | solution.py:40
  74.0 8.0 %copy.70 = bf16[32,256,256]{2,0,1:T(8,128)(2,1)} copy(bf16[32,256,256]{1,2,0:T(8,128)(2,1)} %fusion.3) | data formatting | bytes 8388608 | tf_op jit(solution)/shard_map/convert_element_type | solution.py:41
  82.0 2.7 gather_fusion.4
  84.7 2.8 gather_fusion.5
  87.5 0.1 select_bitcast_fusion.1
  87.6 0.2 copy.71
  87.7 6.7 %collective-permute-start.4 = (bf16[32,16,256]{2,1,0:T(8,128)(2,1)S(1)}, bf16[32,16,256]{2,1,0:T(8,128)(2,1)S(1)}, u32[]{:S(2)}, u32[]{:S(2)}) collective-permute-start(bf16[32,16,256]{2,1,0:T(8,128)(2,1)S(1)} %copy.71), channel_id=1, source_target_pairs={{0,4},{4,8},{8,12},{12,16},{16,20},{20,24},{24,28},{1,5},{5,9},{9,... | collective-permute-start | bytes 786440 | tf_op jit(solution)/shard_map/ppermute | solution.py:19
  94.4 0.1 select_bitcast_fusion
  94.5 0.2 copy.73
  94.7 1.5 collective-permute-start.5
  96.2 0.7 bitcast_or_fusion
  96.9 1.0 copy.74
  97.9 0.2 collective-permute-done.5
  98.1 1.7 copy.75
  99.8 11.1 %multiply_reduce_fusion = (f32[32,256]{1,0:T(8,128)S(1)}, f32[32,256,256]{1,2,0:T(8,128)}) fusion(f32[256]{0:T(256)S(1)} %convert_add_fusion.6, bf16[32,256,256]{1,2,0:T(8,128)(2,1)} %fusion.3, s32[256,288]{0,1:T(8,128)S(1)} %copy-done.3, bf16[32,16,256]{1,2,0:T(8,128)(2,1)} %copy.75, bf16[32,16,256]{1,2,0:T(8,128)(2,1)S(1)} %copy.74), kind=kOutput, calls=%fused_computation.21 | convolution fusion | flops 1232666624 | bytes 13435904 | tf_op jit(solution)/shard_map/nm,cmf->cnf/dot_general | solution.py:37
  111.0 6.8 %fusion.30 = f32[4,32,256]{2,0,1:T(4,128)S(1)} fusion(bf16[32,256,256]{1,2,0:T(8,128)(2,1)} %fusion.3, f32[32,256,256]{1,2,0:T(8,128)} %get-tuple-element.23, f32[32,256]{1,0:T(8,128)S(1)} %add_rsqrt_fusion, bf16[3,256,256]{2,1,0:T(8,128)(2,1)} %param.16, s32[256]{0:T(256)S(1)} %copy-done.5), kind=kOutput, calls=%fused_computation.50 | convolution fusion | flops 1109394432 | bytes 12878848 | tf_op jit(solution)/shard_map/gn,cnf->gcf/dot_general | solution.py:58
  117.8 0.7 copy.81
  118.5 0.1 reshape.197
  118.6 0.3 select_reduce_fusion
  118.9 6.8 %gather_fusion.6 = f32[1024]{0:T(1024)S(1)} fusion(f32[16,128]{1,0:T(8,128)S(1)} %get-tuple-element.25, s32[1024]{0:T(1024)S(1)} %reshape.197), kind=kCustom, calls=%fused_computation.1.clone | custom fusion | bytes 16384 | tf_op jit(solution)/shard_map/jit(take_along_axis)/gather | solution.py:91
  125.7 0.1 reshape.200
  125.8 27.2 %reduce-scatter.2.cloned.1.call-done = f32[16,256]{1,0:T(8,128)} async-done(((f32[128,256]{1,0:T(8,128)}), f32[16,256]{1,0:T(8,128)}) %reduce-scatter.2.cloned.1.call-update) | async-done | bytes 16400 | tf_op jit(solution)/shard_map/reduce_scatter | solution.py:64
  152.9 0.8 multiply_reduce_fusion.3
  153.8 0.8 multiply_convert_fusion.14
  154.6 14.0 %all_gather.6 = bf16[128,256]{1,0:T(8,128)(2,1)S(1)} all-gather(bf16[16,256]{1,0:T(8,128)(2,1)S(1)} %multiply_convert_fusion.14), channel_id=1, replica_groups=mesh['seg'=8,'cfg'=4] {'seg'}, dimensions={0}, use_global_device_ids=true | all-gather | bytes 73728 | tf_op jit(solution)/shard_map/all_gather | solution.py:66
  168.5 0.1 copy.82
  168.6 9.2 %all_gather.7 = bf16[4,128,256]{2,0,1:T(4,128)(2,1)S(1)} all-gather(bf16[4,32,256]{2,0,1:T(4,128)(2,1)S(1)} %copy.82), channel_id=1, replica_groups=mesh['seg'=8,'cfg'=4] {'cfg'}, dimensions={1}, use_global_device_ids=true | all-gather | bytes 327680 | tf_op jit(solution)/shard_map/all_gather | solution.py:68
  177.8 0.5 fusion.67
  178.3 0.1 convolution_bitcast_fusion
  178.5 2.8 fusion.32
  181.3 6.8 %gather_fusion.7 = f32[1024]{0:T(1024)S(1)} fusion(f32[16,128]{1,0:T(8,128)S(1)} %bitcast.86, s32[1024]{0:T(1024)S(1)} %reshape.197), kind=kCustom, calls=%fused_computation.7.clone | custom fusion | bytes 16384 | tf_op jit(solution)/shard_map/jit(take_along_axis)/gather | solution.py:90
  188.1 0.1 reshape.205
  188.2 0.7 fusion.58
  188.9 0.1 multiply_multiply_fusion
  189.0 0.4 convolution_bitcast_fusion.1
  189.4 2.2 fusion.34
  191.7 1.0 fusion.54
  192.7 37.9 %psum.15 = f32[]{:T(128)} all-reduce(f32[]{:T(128)} %get-tuple-element.8), channel_id=1, replica_groups=mesh['seg'=8,'cfg'=4] {'seg','cfg'}, use_global_device_ids=true, to_apply=%region_9.12 | all-reduce | flops 1 | bytes 8 | tf_op jit(solution)/shard_map/psum | solution.py:103
  231.2 84.0 %all-reduce.2.cloned.1.call-done = f32[256,256]{1,0:T(8,128)} async-done(((f32[256,256]{1,0:T(8,128)}), f32[256,256]{1,0:T(8,128)}) %all-reduce.2.cloned.1.call-update) | async-done | bytes 262160 | tf_op jit(solution)/shard_map/psum | solution.py:103
  315.2 0.6 copy.112
  315.9 1.7 copy.113
  (30 shorter events, 0.3 us)
Async XLA Ops:
  7.2 171.2 %copy-start = (bf16[256,256]{1,0:T(8,128)(2,1)S(1)}, bf16[256,256]{1,0:T(8,128)(2,1)}, u32[]{:S(2)}) copy-start(bf16[256,256]{1,0:T(8,128)(2,1)} %param.17) | copy-start | bytes 393220
  7.2 15.1 %copy-start.3 = (s32[256,288]{0,1:T(8,128)S(1)}, s32[256,288]{0,1:T(8,128)}, u32[]{:S(2)}) copy-start(s32[256,288]{0,1:T(8,128)} %param.13) | copy-start | bytes 884740
  7.2 145.7 %reduce-scatter.2.cloned.1.call-start = ((), (), s32[]{:S(2)}) async-start(), calls=%async_computation.1 | async-start | bytes 147456 | tf_op jit(solution)/shard_map/reduce_scatter | solution.py:64
  10.1 12.3 %collective-permute-start = (bf16[32,16,256]{2,1,0:T(8,128)(2,1)S(1)}, bf16[32,16,256]{2,1,0:T(8,128)(2,1)S(1)}, u32[]{:S(2)}, u32[]{:S(2)}) collective-permute-start(bf16[32,16,256]{2,1,0:T(8,128)(2,1)S(1)} %select_bitcast_fusion.5), channel_id=1, source_target_pairs={{0,4},{4,8},{8,12},{12,16},{16,20},{20,24},{24,28},{1,5},{5,9},{9,... | collective-permute-start | bytes 786440 | tf_op jit(solution)/shard_map/ppermute | solution.py:19
  14.6 7.8 %collective-permute-start.1 = (bf16[32,16,256]{2,1,0:T(8,128)(2,1)S(1)}, bf16[32,16,256]{2,1,0:T(8,128)(2,1)S(1)}, u32[]{:S(2)}, u32[]{:S(2)}) collective-permute-start(bf16[32,16,256]{2,1,0:T(8,128)(2,1)S(1)} %select_bitcast_fusion.4), channel_id=1, source_target_pairs={{4,0},{8,4},{12,8},{16,12},{20,16},{24,20},{28,24},{5,1},{9,5},{13... | collective-permute-start | bytes 786440 | tf_op jit(solution)/shard_map/ppermute | solution.py:22
  22.4 5.8 %copy-start.2 = (bf16[32,256,256]{1,2,0:T(8,128)(2,1)S(1)}, bf16[32,256,256]{1,2,0:T(8,128)(2,1)}, u32[]{:S(2)}) copy-start(bf16[32,256,256]{1,2,0:T(8,128)(2,1)} %copy.56) | copy-start | bytes 12582916
  47.4 6.8 %collective-permute-start.2 = (bf16[32,16,256]{2,1,0:T(8,128)(2,1)S(1)}, bf16[32,16,256]{2,1,0:T(8,128)(2,1)S(1)}, u32[]{:S(2)}, u32[]{:S(2)}) collective-permute-start(bf16[32,16,256]{2,1,0:T(8,128)(2,1)S(1)} %copy.61), channel_id=1, source_target_pairs={{0,4},{4,8},{8,12},{12,16},{16,20},{20,24},{24,28},{1,5},{5,9},{9,... | collective-permute-start | bytes 786440 | tf_op jit(solution)/shard_map/ppermute | solution.py:19
  52.9 4.7 %collective-permute-start.3 = (bf16[32,16,256]{2,1,0:T(8,128)(2,1)S(1)}, bf16[32,16,256]{2,1,0:T(8,128)(2,1)S(1)}, u32[]{:S(2)}, u32[]{:S(2)}) collective-permute-start(bf16[32,16,256]{2,1,0:T(8,128)(2,1)S(1)} %copy.63), channel_id=1, source_target_pairs={{4,0},{8,4},{12,8},{16,12},{20,16},{24,20},{28,24},{5,1},{9,5},{13... | collective-permute-start | bytes 786440 | tf_op jit(solution)/shard_map/ppermute | solution.py:22
  59.3 9.2 %copy-start.1 = (bf16[32,256,256]{1,2,0:T(8,128)(2,1)S(1)}, bf16[32,256,256]{1,2,0:T(8,128)(2,1)}, u32[]{:S(2)}) copy-start(bf16[32,256,256]{1,2,0:T(8,128)(2,1)} %fusion.1) | copy-start | bytes 12582916
  87.7 9.2 %collective-permute-start.4 = (bf16[32,16,256]{2,1,0:T(8,128)(2,1)S(1)}, bf16[32,16,256]{2,1,0:T(8,128)(2,1)S(1)}, u32[]{:S(2)}, u32[]{:S(2)}) collective-permute-start(bf16[32,16,256]{2,1,0:T(8,128)(2,1)S(1)} %copy.71), channel_id=1, source_target_pairs={{0,4},{4,8},{8,12},{12,16},{16,20},{20,24},{24,28},{1,5},{5,9},{9,... | collective-permute-start | bytes 786440 | tf_op jit(solution)/shard_map/ppermute | solution.py:19
  94.7 3.4 %collective-permute-start.5 = (bf16[32,16,256]{2,1,0:T(8,128)(2,1)S(1)}, bf16[32,16,256]{2,1,0:T(8,128)(2,1)S(1)}, u32[]{:S(2)}, u32[]{:S(2)}) collective-permute-start(bf16[32,16,256]{2,1,0:T(8,128)(2,1)S(1)} %copy.73), channel_id=1, source_target_pairs={{4,0},{8,4},{12,8},{16,12},{20,16},{24,20},{28,24},{5,1},{9,5},{13... | collective-permute-start | bytes 786440 | tf_op jit(solution)/shard_map/ppermute | solution.py:22
  99.8 11.1 %copy-start.5 = (s32[256]{0:T(256)S(1)}, s32[256]{0:T(256)}, u32[]{:S(2)}) copy-start(s32[256]{0:T(256)} %param.15) | copy-start | bytes 3076
  110.9 7.7 %copy-start.4 = (s32[4,128]{1,0:T(4,128)S(1)}, s32[4,128]{1,0:T(4,128)}, u32[]{:S(2)}) copy-start(s32[4,128]{1,0:T(4,128)} %param.19) | copy-start | bytes 6148
  118.5 196.8 %all-reduce.2.cloned.1.call-start = ((), (), s32[]{:S(2)}) async-start(), calls=%async_computation.2 | async-start | bytes 524288 | tf_op jit(solution)/shard_map/psum | solution.py:103
Sparse Core Ops, SparseCore 0:
  118.6 34.3 reduce-scatter.1
  192.8 122.3 all-reduce.1
where the time goes:
time: 327 us; the launch traced here: 325 us
  waiting for transfers between devices  114 us (35%)
  blocking collectives  61 us (19%)
  local copies, waits for them, and re-layouts  60.3 us (18%)
  matrix products  51.3 us (16%)
  starting transfers between devices  18.4 us (6%)
  between operations  16.2 us (5%)
  other arithmetic  4.59 us (1%)
    psum x1, waiting for transfers between devices, on_device(): weight_grad, loss_total = lax.psum((grad_part, loss_part), ('seg', 'cfg'))  84 us
    psum x1, blocking collectives, on_device(): weight_grad, loss_total = lax.psum((grad_part, loss_part), ('seg', 'cfg'))  37.9 us
    reduce_scatter x1, waiting for transfers between devices, on_device(): lax.psum_scatter(flat_pooled, 'seg', scatter_dimension=0, tiled=True)  27.2 us
    dot_general x3, matrix products, conv_layer(): jnp.einsum('nm,cmf->cnf', adj_weights, extended, preferred_element_type=j...  26 us
    convert_element_type x2, local copies, waits for them, and re-layouts, conv_layer(): (hidden.astype(jnp.float32) + jax.nn.silu(branch)).astype(jnp.bfloat16)  15.9 us
    ppermute x3, starting transfers between devices, with_halo(): lax.ppermute(lax.slice_in_dim(block, block.shape[dim] - width, None, axis...  14.3 us
    all_gather x1, blocking collectives, on_device(): emb_flat = lax.all_gather(own_emb, 'seg', axis=0, tiled=True)  14 us
    dot_general x2, matrix products, conv_layer(): jnp.einsum('cnf,fg->cng', normed, weight, preferred_element_type=jnp.floa...  11 us
  transfers between devices with their start and end apart: 8, of which 4 were waited for; matrix products, arithmetic and copies ran while one was open for 6% of the time, Pallas kernels for 0%

commit v1 on v0

v1 whole, which is shorter than its diff:
```python
import functools

import jax
import jax.numpy as jnp
from jax import lax
from jax.experimental import pallas as pl
from jax.experimental.pallas import tpu as pltpu
from jax.sharding import PartitionSpec as P

P_SIZE = 64
G = 4
eps = 1e-06
MESH = pl.DeviceIdType.MESH
f32, bf16 = jnp.float32, jnp.bfloat16


def dot(a, b):
    return jnp.dot(a, b, preferred_element_type=f32)


def split3(values):
    high = values.astype(bf16)
    rest = values - high.astype(f32)
    middle = rest.astype(bf16)
    low = (rest - middle.astype(f32)).astype(bf16)
    return high, middle, low


def each(count, fn):
    lax.fori_loop(0, count, lambda i, c: (fn(i), c)[1], 0)


def column(row, size):
    rows = lax.broadcasted_iota(jnp.int32, (size, size), 0)
    lanes = lax.broadcasted_iota(jnp.int32, (size, size), 1)
    return jnp.sum(jnp.where(rows == lanes, jnp.broadcast_to(row, (size, size)), 0.0), axis=1, keepdims=True)


def kernel(
    sizes,
    feats, adjacency, halo_rows, node_graph, weights, bilinear, partners, ranking,
    emb_out, grad_out, loss_out,
    ext0, ext1, ext2, outbox, pooled, parts, emb_all, cnt_all, sgn, adj_mat, pick, member, half_w, eps_col,
    in_sem, halo_send, halo_recv, pool_send, pool_recv, seg_send, seg_recv, cfg_send, cfg_recv, cnt_send, cnt_recv,
):
    S, Q, configs, nodes, feat, rim, layers, unroll, own_rows, owners = sizes
    exts = (ext0, ext1, ext2)
    chunks = configs // unroll
    total = Q * configs
    seg, cfg = lax.axis_index("seg"), lax.axis_index("cfg")

    barrier = pltpu.get_barrier_semaphore()

    def greet(axis, me, count):
        def one(k):
            pl.semaphore_signal(barrier, inc=1, device_id={axis: lax.rem(me + k + 1, count)}, device_id_type=MESH)
        each(count - 1, one)

    greet("seg", seg, S)
    greet("cfg", cfg, Q)

    def load(i):
        return pltpu.make_async_copy(
            feats.at[pl.ds(i * unroll, unroll)],
            ext0.at[pl.ds(i * unroll, unroll), pl.ds(rim, nodes)],
            in_sem.at[i],
        )

    each(chunks, lambda i: load(i).start())

    adj = adjacency[...].astype(f32)
    degree = jnp.sum(adj, axis=1, keepdims=True)
    rows = lax.broadcasted_iota(jnp.int32, adj.shape, 0)
    lanes = lax.broadcasted_iota(jnp.int32, adj.shape, 1)
    adj_mat[...] = (adj + jnp.where(lanes == rows + rim, 1.0, 0.0)).astype(bf16)
    eps_col[...] = eps * (1.0 + degree) * (1.0 + degree)
    half_w[...] = (weights[...].astype(f32) * 0.5).astype(bf16)
    node_ids = lax.broadcasted_iota(jnp.int32, (rim, nodes), 1).astype(f32)
    for side in range(2):
        wanted = column(halo_rows[side : side + 1, :].astype(f32), rim)
        pick[side * rim : (side + 1) * rim, :] = jnp.where(node_ids == wanted, 1.0, 0.0).astype(bf16)
    graph_ids = lax.broadcasted_iota(jnp.int32, (16, nodes), 0)
    member[...] = jnp.where(graph_ids == jnp.broadcast_to(node_graph[...], (16, nodes)), 1.0, 0.0).astype(bf16)

    @pl.when(seg == 0)
    def _():
        for ext in exts:
            ext[:, 0:rim, :] = jnp.zeros((configs, rim, feat), bf16)

    @pl.when(seg == S - 1)
    def _():
        for ext in exts:
            ext[:, rim + nodes : 2 * rim + nodes, :] = jnp.zeros((configs, rim, feat), bf16)

    pl.semaphore_wait(barrier, S + Q - 2)

    def halo_copy(l, i, side):
        batch = pl.ds(i * unroll, unroll)
        return pltpu.make_async_remote_copy(
            src_ref=outbox.at[l, batch, pl.ds(side * rim, rim)],
            dst_ref=exts[l].at[batch, pl.ds(0 if side else rim + nodes, rim)],
            send_sem=halo_send.at[l, side, i],
            recv_sem=halo_recv.at[l, side, i],
            device_id={"seg": seg + 1 if side else seg - 1},
            device_id_type=MESH,
        )

    def halo_each(l, i, sends, act):
        up, down = seg < S - 1, seg > 0

        @pl.when(down if sends else up)
        def _():
            act(halo_copy(l, i, 0))

        @pl.when(up if sends else down)
        def _():
            act(halo_copy(l, i, 1))

    def first(i):
        load(i).wait()
        for u in range(unroll):
            c = i * unroll + u
            outbox[0, c] = dot(pick[...], ext0[c, rim : rim + nodes, :]).astype(bf16)
        halo_each(0, i, True, lambda copy: copy.start())

    each(chunks, first)

    def layer(l, i):
        halo_each(l, i, False, lambda copy: copy.wait_recv())
        for u in range(unroll):
            c = i * unroll + u
            summed = dot(adj_mat[...], exts[l][c])
            square = jnp.sum(summed * summed, axis=1, keepdims=True) * (1.0 / feat)
            normed = (summed * lax.rsqrt(square + eps_col[...])).astype(bf16)
            half = dot(normed, half_w[l])
            before = exts[l][c, rim : rim + nodes, :].astype(f32)
            hidden = (before + (half + half * jnp.tanh(half))).astype(bf16)
            if l < layers - 1:
                exts[l + 1][c, rim : rim + nodes, :] = hidden
                outbox[l + 1, c] = dot(pick[...], hidden).astype(bf16)
            else:
                sums = dot(member[...], hidden)
                for g in range(G):
                    pooled[pl.ds(g * configs + c, 1), :] = sums[g : g + 1, :]
        if l < layers - 1:
            halo_each(l + 1, i, True, lambda copy: copy.start())

    for l in range(layers - 1):
        each(chunks, functools.partial(layer, l))

    def pool_copy(source, o):
        return pltpu.make_async_remote_copy(
            src_ref=pooled.at[pl.ds(o * own_rows, own_rows)],
            dst_ref=parts.at[source],
            send_sem=pool_send.at[o],
            recv_sem=pool_recv.at[source],
            device_id={"seg": o},
            device_id_type=MESH,
        )

    groups = max(1, configs // own_rows)
    per_group = chunks // groups

    def last_group(p):
        each(per_group, lambda j: layer(layers - 1, p * per_group + j))

        def send(k):
            o = k * groups + p

            @pl.when(o != seg)
            def _():
                pool_copy(seg, o).start()

        each(owners // groups, send)

    each(groups, last_group)

    block = 16 if (G * configs) % 16 == 0 else 8

    def count(r):
        where = pl.ds(pl.multiple_of(r * block, block), block)
        chosen = partners[where, :]
        ids = lax.broadcasted_iota(jnp.int32, (block, total), 1)
        found = jnp.zeros((block, total), f32)
        for k in range(P_SIZE):
            found = found + jnp.where(chosen[:, k : k + 1] == ids, 1.0, 0.0)
        cnt_all[cfg, where, :] = found.astype(bf16)

    each(G * configs // block, count)

    def cnt_copy(d):
        return pltpu.make_async_remote_copy(
            src_ref=cnt_all.at[cfg],
            dst_ref=cnt_all.at[cfg],
            send_sem=cnt_send.at[d],
            recv_sem=cnt_recv.at[d],
            device_id={"cfg": lax.rem(cfg + d + 1, Q)},
            device_id_type=MESH,
        )

    each(Q - 1, lambda d: cnt_copy(d).start())

    for g in range(G):
        theirs = jnp.broadcast_to(ranking[g : g + 1, :].astype(f32), (total, total))
        ahead = theirs - column(ranking[g : g + 1, :].astype(f32), total)
        sgn[g] = jnp.where(ahead > 0.0, 1.0, jnp.where(ahead < 0.0, -1.0, 0.0))

    def emb_block(q, o):
        return emb_all.at[q, pl.ds(o * own_rows, own_rows)]

    def seg_copy(k, o):
        return pltpu.make_async_remote_copy(
            src_ref=emb_block(cfg, o),
            dst_ref=emb_block(cfg, o),
            send_sem=seg_send.at[k],
            recv_sem=seg_recv.at[o],
            device_id={"seg": lax.rem(seg + k + 1, S)},
            device_id_type=MESH,
        )

    def cfg_copy(d, q, o):
        return pltpu.make_async_remote_copy(
            src_ref=emb_block(q, o),
            dst_ref=emb_block(q, o),
            send_sem=cfg_send.at[d, o],
            recv_sem=cfg_recv.at[d, o],
            device_id={"cfg": lax.rem(cfg + d + 1, Q)},
            device_id_type=MESH,
        )

    @pl.when(seg < owners)
    def _():
        parts[seg] = pooled[pl.ds(pl.multiple_of(seg * own_rows, own_rows), own_rows), :]

        def arrive(k):
            pool_copy(lax.rem(seg + k + 1, S), seg).wait_recv()

        each(S - 1, arrive)
        summed = parts[0]
        for s in range(1, S):
            summed = summed + parts[s]
        square = jnp.sum(summed * summed, axis=1, keepdims=True) * (1.0 / feat)
        mine = pl.ds(pl.multiple_of(seg * own_rows, own_rows), own_rows)
        emb_all[cfg, mine, :] = (summed * lax.rsqrt(square + eps)).astype(bf16)
        each(S - 1, lambda k: seg_copy(k, seg).start())

    def forward(k):
        o = lax.rem(seg + k, owners)

        @pl.when(o != seg)
        def _():
            seg_copy(0, o).wait_recv()

        each(Q - 1, lambda d: cfg_copy(d, cfg, o).start())

    each(owners, forward)

    for l in range(layers):
        each(chunks, lambda i: halo_each(l, i, True, lambda copy: copy.wait_send()))

    def sent(o):
        @pl.when(o != seg)
        def _():
            pool_copy(seg, o).wait_send()

    each(owners, sent)

    @pl.when(seg < owners)
    def _():
        each(S - 1, lambda k: seg_copy(k, seg).wait_send())

    each(Q - 1, lambda d: cnt_copy(d).wait())

    def arrived(d):
        source = lax.rem(cfg + Q - d - 1, Q)
        each(owners, lambda o: cfg_copy(d, source, o).wait_recv())

    each(Q - 1, arrived)
    emb_out[...] = emb_all[cfg]

    def of_graph(ref, g):
        if configs % 16 == 0:
            rows = ref[:, g * configs : (g + 1) * configs, :]
        else:
            rows = ref[...].astype(f32)[:, g * configs : (g + 1) * configs, :]
        return rows.reshape(total, rows.shape[2]).astype(bf16)

    grad = jnp.zeros((feat, feat), f32)
    loss = jnp.zeros((1, 1), f32)
    for g in range(G):
        emb = of_graph(emb_all, g)
        often = of_graph(cnt_all, g).astype(f32)
        emb_t = emb.astype(f32).T.astype(bf16)
        projected = dot(emb, bilinear[...])
        stacked = dot(jnp.concatenate(split3(projected), axis=0), emb_t)
        scores = stacked[:total] + stacked[total : 2 * total] + stacked[2 * total :]
        sign = sgn[g]
        margin = 1.0 - sign * scores
        decay = jnp.exp(-jnp.abs(margin))
        soft = jnp.maximum(margin, 0.0) + jnp.log1p(decay)
        sigmoid = jnp.where(margin >= 0.0, 1.0, decay) / (1.0 + decay)
        loss = loss + jnp.sum(often * soft, axis=(0, 1), keepdims=True)
        coef = often * (-sign) * sigmoid * (1.0 / (G * P_SIZE))
        stacked = dot(jnp.concatenate(split3(coef), axis=0), emb)
        carried = stacked[:total] + stacked[total : 2 * total] + stacked[2 * total :]
        high, middle, low = split3(carried)
        grad = grad + (dot(emb_t, high) + dot(emb_t, middle) + dot(emb_t, low))
    grad_out[...] = grad
    loss_out[...] = loss * (1.0 / (G * total * P_SIZE))

    def cfg_sent(d):
        each(owners, lambda o: cfg_copy(d, cfg, o).wait_send())

    each(Q - 1, cfg_sent)


def on_device(S, Q, node_feats, adjacency, halo_rows, node_graph, layer_weights, bilinear, partners, ranking):
    configs, nodes, feat = node_feats.shape
    rim, layers = halo_rows.shape[2], layer_weights.shape[0]
    unroll = 4
    chunks = configs // unroll
    own_rows = max(16, G * configs // S)
    owners = G * configs // own_rows
    total = Q * configs
    wide = nodes + 2 * rim
    sizes = (S, Q, configs, nodes, feat, rim, layers, unroll, own_rows, owners)
    vmem = pl.BlockSpec(memory_space=pltpu.VMEM)
    dma = pltpu.SemaphoreType.DMA
    emb, grad, loss = pl.pallas_call(
        functools.partial(kernel, sizes),
        out_shape=(
            jax.ShapeDtypeStruct((G * configs, feat), bf16),
            jax.ShapeDtypeStruct((feat, feat), f32),
            jax.ShapeDtypeStruct((1, 1), f32),
        ),
        in_specs=[pl.BlockSpec(memory_space=pl.ANY)] + [vmem] * 7,
        out_specs=(vmem, vmem, vmem),
        scratch_shapes=[pltpu.VMEM((configs, wide, feat), bf16)] * 3
        + [
            pltpu.VMEM((layers, configs, 2 * rim, feat), bf16),
            pltpu.VMEM((G * configs, feat), f32),
            pltpu.VMEM((S, own_rows, feat), f32),
            pltpu.VMEM((Q, G * configs, feat), bf16),
            pltpu.VMEM((Q, G * configs, total), bf16),
            pltpu.VMEM((G, total, total), f32),
            pltpu.VMEM((nodes, wide), bf16),
            pltpu.VMEM((2 * rim, nodes), bf16),
            pltpu.VMEM((16, nodes), bf16),
            pltpu.VMEM((layers, feat, feat), bf16),
            pltpu.VMEM((nodes, 1), f32),
            dma((chunks,)),
            dma((layers, 2, chunks)),
            dma((layers, 2, chunks)),
            dma((owners,)),
            dma((S,)),
            dma((S - 1,)),
            dma((owners,)),
            dma((Q - 1, owners)),
            dma((Q - 1, owners)),
            dma((Q - 1,)),
            dma((Q - 1,)),
        ],
        compiler_params=pltpu.CompilerParams(
            collective_id=0, has_side_effects=True, vmem_limit_bytes=48 * 1024 * 1024
        ),
    )(
        node_feats,
        adjacency,
        halo_rows.reshape(2, rim),
        node_graph.reshape(1, nodes),
        layer_weights,
        bilinear,
        partners.reshape(G * configs, partners.shape[2]),
        ranking,
    )
    return emb.reshape(G, configs, feat), grad, loss.reshape(())


def solution(mesh):
    placed = (
        P("cfg", "seg", None),
        P("seg", None),
        P("seg", None, None),
        P("seg"),
        P(),
        P(),
        P(None, "cfg", None),
        P(),
    )
    return jax.shard_map(
        functools.partial(on_device, mesh.shape["seg"], mesh.shape["cfg"]),
        mesh=mesh,
        in_specs=placed,
        out_specs=(P(None, "cfg", None), P(), P()),
        check_vma=False,
    )
```

time: 327 us -> 98.1 us (0.30)
  waiting for transfers between devices: 114 us -> 0 us
  Pallas kernels: 0 us -> 86 us
  blocking collectives: 61 us -> 0 us
  matrix products: 51.3 us -> 0 us
  local copies, waits for them, and re-layouts: 60.3 us -> 9.42 us
  starting transfers between devices: 18.4 us -> 0 us
  between operations: 16.2 us -> 2.35 us
  other arithmetic: 4.59 us -> 0 us
    pallas_call x0 -> x1, Pallas kernels: none -> 86 us  [on_device(): pl.pallas_call(functools.partial(kernel, sizes), out_shape=(jax.ShapeDtyp...]
    psum x1 -> x0, waiting for transfers between devices: 84 us -> none  [on_device(): weight_grad, loss_total = lax.psum((grad_part, loss_part), ('seg', 'cfg'))]
    dot_general x13 -> x0, matrix products: 51.3 us -> none  [the longest x3 26 us: conv_layer(): jnp.einsum('nm,cmf->cnf', adj_weights, extended, preferred_element_type=j...]
    psum x1 -> x0, blocking collectives: 37.9 us -> none  [on_device(): weight_grad, loss_total = lax.psum((grad_part, loss_part), ('seg', 'cfg'))]
    gather x11 -> x0, local copies, waits for them, and re-layouts: 28.8 us -> none  [the longest x3 7.49 us: conv_layer(): jnp.take(hidden, own_halo[0], axis=1)]
    reduce_scatter x1 -> x0, waiting for transfers between devices: 27.2 us -> none  [on_device(): lax.psum_scatter(flat_pooled, 'seg', scatter_dimension=0, tiled=True)]
    all_gather x2 -> x0, blocking collectives: 23.2 us -> none  [the longest x1 14 us: on_device(): emb_flat = lax.all_gather(own_emb, 'seg', axis=0, tiled=True)]
    ppermute x6 -> x0, starting transfers between devices: 18.3 us -> none  [the longest x3 14.3 us: with_halo(): lax.ppermute(lax.slice_in_dim(block, block.shape[dim] - width, None, axis...]
  transfers between devices with their start and end apart: 8 -> 0, of which waited for: 4 -> 0; matrix products, arithmetic and copies ran while one was open for 6% -> 0% of each run, Pallas kernels for 0% -> 0%
where the time goes in v1:
time: 98.1 us; the launch traced here: 97.8 us
  Pallas kernels  86 us (88%)
  local copies, waits for them, and re-layouts  9.42 us (10%)
  between operations  2.35 us (2%)
    pallas_call x1, Pallas kernels, on_device(): pl.pallas_call(functools.partial(kernel, sizes), out_shape=(jax.ShapeDtyp...  86 us
    unnamed x17, local copies, waits for them, and re-layouts  9.42 us

profile of v1, /device:TPU:0, one launch (start us, length us, event | category | flops | bytes accessed | tf_op | source)
XLA Modules:
  0.0 97.8 jit_solution(17411500583614718101)
XLA Ops:
  0.6 1.1 %copy.11.adjacency = s32[256,288]{1,0:T(8,128)S(1)} copy(s32[256,288]{0,1:T(8,128)} %param.9) | data formatting | bytes 589824 | tf_op args[1]
  1.8 0.0 copy-start
  1.8 2.2 %copy-done = bf16[32,256,256]{2,1,0:T(8,128)(2,1)S(1)} copy-done((bf16[32,256,256]{2,1,0:T(8,128)(2,1)S(1)}, bf16[32,256,256]{2,1,0:T(8,128)(2,1)}, u32[]{:S(2)}) %copy-start) | copy-done | bytes 4194328
  4.0 0.0 copy-start.1
  4.0 1.0 %copy-done.1 = bf16[3,256,256]{2,1,0:T(8,128)(2,1)S(1)} copy-done((bf16[3,256,256]{2,1,0:T(8,128)(2,1)S(1)}, bf16[3,256,256]{2,1,0:T(8,128)(2,1)}, u32[]{:S(2)}) %copy-start.1) | copy-done | bytes 393240
  4.9 0.0 copy-start.2
  5.0 0.9 copy-done.2
  5.9 0.0 copy-start.3
  5.9 0.8 copy-done.3
  6.7 0.0 copy-start.4
  6.7 0.7 copy-done.4
  7.4 0.0 copy-start.5
  7.4 0.7 copy-done.5
  8.1 0.0 copy-start.6
  8.1 0.7 copy-done.6
  8.7 86.0 %shard_map.103 = (bf16[128,256]{1,0:T(8,128)(2,1)S(1)}, f32[256,256]{1,0:T(8,128)S(1)}, f32[1,1]{1,0:T(1,128)}) custom-call(bf16[32,256,256]{2,1,0:T(8,128)(2,1)S(1)} %copy-done, s32[256,288]{1,0:T(8,128)S(1)} %copy.11.adjacency, s32[2,16]{1,0:T(2,128)S(1)} %bitcast.7, s32[1,256]{1,0:T(1,128)S(1)} %bitcast.8, bf16[3,256,256]{2,1,0:T(8,128)(2,1)S(1)} %copy-done.1, ...), custom_call_target="tpu_custom_call" | custom-call | tf_op jit(solution)/shard_map/pallas_call | solution.py:329
  94.8 0.6 copy.15
  95.4 0.7 copy.16
Async XLA Ops:
  1.8 2.2 %copy-start = (bf16[32,256,256]{2,1,0:T(8,128)(2,1)S(1)}, bf16[32,256,256]{2,1,0:T(8,128)(2,1)}, u32[]{:S(2)}) copy-start(bf16[32,256,256]{2,1,0:T(8,128)(2,1)} %feats.1) | copy-start | bytes 12582916
  4.0 1.0 %copy-start.1 = (bf16[3,256,256]{2,1,0:T(8,128)(2,1)S(1)}, bf16[3,256,256]{2,1,0:T(8,128)(2,1)}, u32[]{:S(2)}) copy-start(bf16[3,256,256]{2,1,0:T(8,128)(2,1)} %weights.1) | copy-start | bytes 1179652
  4.9 0.9 copy-start.2
  5.9 0.8 copy-start.3
  6.7 0.7 copy-start.4
  7.4 0.7 copy-start.5
  8.1 0.7 copy-start.6

commit v2 on v1

--- a/solution.py
+++ b/solution.py
@@ -9,6 +9,7 @@
 
 P_SIZE = 64
 G = 4
+LANES = 128
 eps = 1e-06
 MESH = pl.DeviceIdType.MESH
 f32, bf16 = jnp.float32, jnp.bfloat16
@@ -38,9 +39,16 @@
 
 def kernel(
     sizes,
-    feats, adjacency, halo_rows, node_graph, weights, bilinear, partners, ranking,
+    feats, *rest,
+):
+    compute(sizes, feats, rest[:7], *rest[7:])
+
+
+def compute(
+    sizes, feats, sources,
     emb_out, grad_out, loss_out,
-    ext0, ext1, ext2, outbox, pooled, parts, emb_all, cnt_all, sgn, adj_mat, pick, member, half_w, eps_col,
+    ext0, ext1, ext2, outbox, pooled, parts, emb_all, cnt_all, sgn, adj_mat, pick, member, half_w, eps_wide,
+    adjacency, halo_rows, node_graph, weights, bilinear, partners, ranking, small_sem,
     in_sem, halo_send, halo_recv, pool_send, pool_recv, seg_send, seg_recv, cfg_send, cfg_recv, cnt_send, cnt_recv,
 ):
     S, Q, configs, nodes, feat, rim, layers, unroll, own_rows, owners = sizes
@@ -59,6 +67,15 @@
     greet("seg", seg, S)
     greet("cfg", cfg, Q)
 
+    copies = [
+        pltpu.make_async_copy(source, target, small_sem.at[n])
+        for n, (source, target) in enumerate(
+            zip(sources, (adjacency, halo_rows, node_graph, weights, bilinear, partners, ranking))
+        )
+    ]
+    for copy in copies:
+        copy.start()
+
     def load(i):
         return pltpu.make_async_copy(
             feats.at[pl.ds(i * unroll, unroll)],
@@ -68,12 +85,17 @@
 
     each(chunks, lambda i: load(i).start())
 
-    adj = adjacency[...].astype(f32)
+    for copy in copies:
+        copy.wait()
+    wide = nodes + 2 * rim
+    padded = -(-wide // LANES) * LANES
+    turned = jnp.concatenate([adjacency[...].astype(f32), jnp.zeros((padded - wide, nodes), f32)], axis=0)
+    adj = turned.T[:, :wide]
     degree = jnp.sum(adj, axis=1, keepdims=True)
     rows = lax.broadcasted_iota(jnp.int32, adj.shape, 0)
     lanes = lax.broadcasted_iota(jnp.int32, adj.shape, 1)
     adj_mat[...] = (adj + jnp.where(lanes == rows + rim, 1.0, 0.0)).astype(bf16)
-    eps_col[...] = eps * (1.0 + degree) * (1.0 + degree)
+    eps_wide[...] = jnp.broadcast_to(eps * (1.0 + degree) * (1.0 + degree), (nodes, LANES))
     half_w[...] = (weights[...].astype(f32) * 0.5).astype(bf16)
     node_ids = lax.broadcasted_iota(jnp.int32, (rim, nodes), 1).astype(f32)
     for side in range(2):
@@ -118,30 +140,41 @@
 
     def first(i):
         load(i).wait()
-        for u in range(unroll):
-            c = i * unroll + u
-            outbox[0, c] = dot(pick[...], ext0[c, rim : rim + nodes, :]).astype(bf16)
+        ids = [i * unroll + u for u in range(unroll)]
+        blocks = [ext0[c, rim : rim + nodes, :] for c in ids]
+        picked = [dot(pick[...], block).astype(bf16) for block in blocks]
+        for c, rows in zip(ids, picked):
+            outbox[0, c] = rows
         halo_each(0, i, True, lambda copy: copy.start())
 
     each(chunks, first)
 
     def layer(l, i):
         halo_each(l, i, False, lambda copy: copy.wait_recv())
+        ids = [i * unroll + u for u in range(unroll)]
+        before = [exts[l][c] for c in ids]
+        summed = [dot(adj_mat[...], block) for block in before]
+        normed = []
+        for values in summed:
+            square = jnp.sum(values * values, axis=1, keepdims=True) * (1.0 / feat)
+            scale = lax.rsqrt(jnp.broadcast_to(square, eps_wide.shape) + eps_wide[...])
+            normed.append((values * jnp.tile(scale, (1, feat // LANES))).astype(bf16))
+        halves = dot(jnp.concatenate(normed, axis=0), half_w[l])
+        hidden = []
         for u in range(unroll):
-            c = i * unroll + u
-            summed = dot(adj_mat[...], exts[l][c])
-            square = jnp.sum(summed * summed, axis=1, keepdims=True) * (1.0 / feat)
-            normed = (summed * lax.rsqrt(square + eps_col[...])).astype(bf16)
-            half = dot(normed, half_w[l])
-            before = exts[l][c, rim : rim + nodes, :].astype(f32)
-            hidden = (before + (half + half * jnp.tanh(half))).astype(bf16)
-            if l < layers - 1:
-                exts[l + 1][c, rim : rim + nodes, :] = hidden
-                outbox[l + 1, c] = dot(pick[...], hidden).astype(bf16)
-            else:
-                sums = dot(member[...], hidden)
+            half = halves[u * nodes : (u + 1) * nodes]
+            own = before[u][rim : rim + nodes].astype(f32)
+            hidden.append((own + (half + half * jnp.tanh(half))).astype(bf16))
+        if l < layers - 1:
+            picked = [dot(pick[...], values).astype(bf16) for values in hidden]
+            for c, values, rows in zip(ids, hidden, picked):
+                exts[l + 1][c, rim : rim + nodes, :] = values
+                outbox[l + 1, c] = rows
+        else:
+            sums = [dot(member[...], values) for values in hidden]
+            for c, values in zip(ids, sums):
                 for g in range(G):
-                    pooled[pl.ds(g * configs + c, 1), :] = sums[g : g + 1, :]
+                    pooled[pl.ds(g * configs + c, 1), :] = values[g : g + 1, :]
         if l < layers - 1:
             halo_each(l + 1, i, True, lambda copy: copy.start())
 
@@ -333,7 +366,7 @@
             jax.ShapeDtypeStruct((feat, feat), f32),
             jax.ShapeDtypeStruct((1, 1), f32),
         ),
-        in_specs=[pl.BlockSpec(memory_space=pl.ANY)] + [vmem] * 7,
+        in_specs=[pl.BlockSpec(memory_space=pl.ANY)] * 8,
         out_specs=(vmem, vmem, vmem),
         scratch_shapes=[pltpu.VMEM((configs, wide, feat), bf16)] * 3
         + [
@@ -347,7 +380,15 @@
             pltpu.VMEM((2 * rim, nodes), bf16),
             pltpu.VMEM((16, nodes), bf16),
             pltpu.VMEM((layers, feat, feat), bf16),
-            pltpu.VMEM((nodes, 1), f32),
+            pltpu.VMEM((nodes, LANES), f32),
+            pltpu.VMEM((wide, nodes), jnp.int32),
+            pltpu.VMEM((2, rim), jnp.int32),
+            pltpu.VMEM((1, nodes), jnp.int32),
+            pltpu.VMEM((layers, feat, feat), bf16),
+            pltpu.VMEM((feat, feat), bf16),
+            pltpu.VMEM((G * configs, partners.shape[2]), jnp.int32),
+            pltpu.VMEM((G, total), jnp.int32),
+            dma((7,)),
             dma((chunks,)),
             dma((layers, 2, chunks)),
             dma((layers, 2, chunks)),
@@ -361,11 +402,11 @@
             dma((Q - 1,)),
         ],
         compiler_params=pltpu.CompilerParams(
-            collective_id=0, has_side_effects=True, vmem_limit_bytes=48 * 1024 * 1024
+            collective_id=0, has_side_effects=True, vmem_limit_bytes=63 * 1024 * 1024
         ),
     )(
         node_feats,
-        adjacency,
+        adjacency.T,
         halo_rows.reshape(2, rim),
         node_graph.reshape(1, nodes),
         layer_weights,

time: 98.1 us -> 49.9 us (0.51)
  Pallas kernels: 86 us -> 44.2 us
  local copies, waits for them, and re-layouts: 9.42 us -> 3.14 us
    pallas_call x1, Pallas kernels: 86 us -> 44.2 us  [on_device(): pl.pallas_call(functools.partial(kernel, sizes), out_shape=(jax.ShapeDtyp...]
    unnamed x17 -> x2, local copies, waits for them, and re-layouts: 9.42 us -> 3.14 us
where the time goes in v2:
time: 49.9 us; the launch traced here: 49.7 us
  Pallas kernels  44.2 us (89%)
  local copies, waits for them, and re-layouts  3.14 us (6%)
  between operations  2.33 us (5%)
    pallas_call x1, Pallas kernels, on_device(): pl.pallas_call(functools.partial(kernel, sizes), out_shape=(jax.ShapeDtyp...  44.2 us
    unnamed x2, local copies, waits for them, and re-layouts  3.14 us

profile of v2, /device:TPU:0, one launch (start us, length us, event | category | flops | bytes accessed | tf_op | source)
XLA Modules:
  0.0 49.7 jit_solution(4573871069109938283)
XLA Ops:
  0.6 44.2 %shard_map.103 = (bf16[128,256]{1,0:T(8,128)(2,1)}, f32[256,256]{1,0:T(8,128)}, f32[1,1]{1,0:T(1,128)}) custom-call(bf16[32,256,256]{2,1,0:T(8,128)(2,1)} %feats.1, s32[288,256]{1,0:T(8,128)} %bitcast.6, s32[2,16]{1,0:T(2,128)} %bitcast.9, s32[1,256]{1,0:T(1,128)} %bitcast.10, bf16[3,256,256]{2,1,0:T(8,128)(2,1)} %rest_3_.1, bf16[256,256]{1,0:T(8,128)(2,1)} %rest_4_.1, ...), custom_call_target="tpu_custom_call" | custom-call | tf_op jit(solution)/shard_map/pallas_call | solution.py:362
  44.8 1.5 %copy.14 = bf16[4,32,256]{2,1,0:T(8,128)(2,1)} copy(bf16[4,32,256]{2,1,0:T(8,128)(2,1)} %bitcast.8) | data formatting | bytes 131072
  46.3 1.7 %copy.15 = f32[256,256]{1,0:T(8,128)} copy(f32[256,256]{1,0:T(8,128)} %get-tuple-element.13) | data formatting | bytes 524288

commit v3 on v2

--- a/solution.py
+++ b/solution.py
@@ -350,7 +350,7 @@
 def on_device(S, Q, node_feats, adjacency, halo_rows, node_graph, layer_weights, bilinear, partners, ranking):
     configs, nodes, feat = node_feats.shape
     rim, layers = halo_rows.shape[2], layer_weights.shape[0]
-    unroll = 4
+    unroll = 8 if configs % 8 == 0 else 4
     chunks = configs // unroll
     own_rows = max(16, G * configs // S)
     owners = G * configs // own_rows

time: 49.9 us -> 47.5 us (0.952)
  Pallas kernels: 44.2 us -> 41.8 us
    pallas_call x1, Pallas kernels: 44.2 us -> 41.8 us  [on_device(): pl.pallas_call(functools.partial(kernel, sizes), out_shape=(jax.ShapeDtyp...]
where the time goes in v3:
time: 47.5 us; the launch traced here: 47.3 us
  Pallas kernels  41.8 us (88%)
  local copies, waits for them, and re-layouts  3.14 us (7%)
  between operations  2.33 us (5%)
    pallas_call x1, Pallas kernels, on_device(): pl.pallas_call(functools.partial(kernel, sizes), out_shape=(jax.ShapeDtyp...  41.8 us
    unnamed x2, local copies, waits for them, and re-layouts  3.14 us

profile of v3, /device:TPU:0, one launch (start us, length us, event | category | flops | bytes accessed | tf_op | source)
XLA Modules:
  0.0 47.3 jit_solution(3966038644783870680)
XLA Ops:
  0.6 41.8 %shard_map.103 = (bf16[128,256]{1,0:T(8,128)(2,1)}, f32[256,256]{1,0:T(8,128)}, f32[1,1]{1,0:T(1,128)}) custom-call(bf16[32,256,256]{2,1,0:T(8,128)(2,1)} %feats.1, s32[288,256]{1,0:T(8,128)} %bitcast.6, s32[2,16]{1,0:T(2,128)} %bitcast.9, s32[1,256]{1,0:T(1,128)} %bitcast.10, bf16[3,256,256]{2,1,0:T(8,128)(2,1)} %rest_3_.1, bf16[256,256]{1,0:T(8,128)(2,1)} %rest_4_.1, ...), custom_call_target="tpu_custom_call" | custom-call | tf_op jit(solution)/shard_map/pallas_call | solution.py:362
  42.5 1.5 %copy.14 = bf16[4,32,256]{2,1,0:T(8,128)(2,1)} copy(bf16[4,32,256]{2,1,0:T(8,128)(2,1)} %bitcast.8) | data formatting | bytes 131072
  43.9 1.7 %copy.15 = f32[256,256]{1,0:T(8,128)} copy(f32[256,256]{1,0:T(8,128)} %get-tuple-element.13) | data formatting | bytes 524288

commit v4 on v3

--- a/solution.py
+++ b/solution.py
@@ -238,6 +238,9 @@
         ahead = theirs - column(ranking[g : g + 1, :].astype(f32), total)
         sgn[g] = jnp.where(ahead > 0.0, 1.0, jnp.where(ahead < 0.0, -1.0, 0.0))
 
+    for l in range(layers):
+        each(chunks, lambda i: halo_each(l, i, True, lambda copy: copy.wait_send()))
+
     def emb_block(q, o):
         return emb_all.at[q, pl.ds(o * own_rows, own_rows)]
 
@@ -277,9 +280,7 @@
         emb_all[cfg, mine, :] = (summed * lax.rsqrt(square + eps)).astype(bf16)
         each(S - 1, lambda k: seg_copy(k, seg).start())
 
-    def forward(k):
-        o = lax.rem(seg + k, owners)
-
+    def forward(o):
         @pl.when(o != seg)
         def _():
             seg_copy(0, o).wait_recv()
@@ -288,28 +289,21 @@
 
     each(owners, forward)
 
-    for l in range(layers):
-        each(chunks, lambda i: halo_each(l, i, True, lambda copy: copy.wait_send()))
+    emb_out[...] = emb_all[cfg]
 
     def sent(o):
         @pl.when(o != seg)
         def _():
             pool_copy(seg, o).wait_send()
 
-    each(owners, sent)
-
-    @pl.when(seg < owners)
-    def _():
-        each(S - 1, lambda k: seg_copy(k, seg).wait_send())
-
     each(Q - 1, lambda d: cnt_copy(d).wait())
 
-    def arrived(d):
-        source = lax.rem(cfg + Q - d - 1, Q)
-        each(owners, lambda o: cfg_copy(d, source, o).wait_recv())
-
-    each(Q - 1, arrived)
-    emb_out[...] = emb_all[cfg]
+    def arrived(first, last):
+        def one(d):
+            source = lax.rem(cfg + Q - d - 1, Q)
+            each(last - first, lambda k: cfg_copy(d, source, first + k).wait_recv())
+
+        each(Q - 1, one)
 
     def of_graph(ref, g):
         if configs % 16 == 0:
@@ -320,7 +314,12 @@
 
     grad = jnp.zeros((feat, feat), f32)
     loss = jnp.zeros((1, 1), f32)
+    paired = (2 * configs) % own_rows == 0
+    if not paired:
+        arrived(0, owners)
     for g in range(G):
+        if paired and g % 2 == 0:
+            arrived(g * configs // own_rows, (g + 2) * configs // own_rows)
         emb = of_graph(emb_all, g)
         often = of_graph(cnt_all, g).astype(f32)
         emb_t = emb.astype(f32).T.astype(bf16)
@@ -345,6 +344,22 @@
         each(owners, lambda o: cfg_copy(d, cfg, o).wait_send())
 
     each(Q - 1, cfg_sent)
+    each(owners, sent)
+
+    @pl.when(seg < owners)
+    def _():
+        each(S - 1, lambda k: seg_copy(k, seg).wait_send())
+
+
+def hand_over(emb, grad, emb_out, grad_out, sems):
+    moves = [
+        pltpu.make_async_copy(emb, emb_out, sems.at[0]),
+        pltpu.make_async_copy(grad, grad_out, sems.at[1]),
+    ]
+    for move in moves:
+        move.start()
+    for move in moves:
+        move.wait()
 
 
 def on_device(S, Q, node_feats, adjacency, halo_rows, node_graph, layer_weights, bilinear, partners, ranking):
@@ -414,6 +429,15 @@
         partners.reshape(G * configs, partners.shape[2]),
         ranking,
     )
+    any_space = pl.BlockSpec(memory_space=pl.ANY)
+    emb, grad = pl.pallas_call(
+        hand_over,
+        out_shape=(jax.ShapeDtypeStruct(emb.shape, bf16), jax.ShapeDtypeStruct(grad.shape, f32)),
+        in_specs=[any_space] * 2,
+        out_specs=(any_space, any_space),
+        scratch_shapes=[dma((2,))],
+        compiler_params=pltpu.CompilerParams(vmem_limit_bytes=63 * 1024 * 1024),
+    )(emb, grad)
     return emb.reshape(G, configs, feat), grad, loss.reshape(())
 
 

time: 47.5 us -> 54.6 us (1.15)
  Pallas kernels: 41.8 us -> 52 us
  local copies, waits for them, and re-layouts: 3.14 us -> 0 us
    pallas_call x0 -> x1, Pallas kernels: none -> 11 us  [on_device(): pl.pallas_call(hand_over, out_shape=(jax.ShapeDtypeStruct(emb.shape, bf16...]
    unnamed x2 -> x0, local copies, waits for them, and re-layouts: 3.14 us -> none
    pallas_call x1, Pallas kernels: 41.8 us -> 41 us  [on_device(): pl.pallas_call(functools.partial(kernel, sizes), out_shape=(jax.ShapeDtyp...]
where the time goes in v4:
time: 54.6 us; the launch traced here: 54.4 us
  Pallas kernels  52 us (95%)
  between operations  2.4 us (4%)
    pallas_call x1, Pallas kernels, on_device(): pl.pallas_call(functools.partial(kernel, sizes), out_shape=(jax.ShapeDtyp...  41 us
    pallas_call x1, Pallas kernels, on_device(): pl.pallas_call(hand_over, out_shape=(jax.ShapeDtypeStruct(emb.shape, bf16...  11 us

profile of v4, /device:TPU:0, one launch (start us, length us, event | category | flops | bytes accessed | tf_op | source)
XLA Modules:
  0.0 54.4 jit_solution(16436818417260456712)
XLA Ops:
  0.6 41.0 %shard_map.103 = (bf16[128,256]{1,0:T(8,128)(2,1)}, f32[256,256]{1,0:T(8,128)}, f32[1,1]{1,0:T(1,128)}) custom-call(bf16[32,256,256]{2,1,0:T(8,128)(2,1)} %feats.1, s32[288,256]{1,0:T(8,128)} %bitcast.6, s32[2,16]{1,0:T(2,128)} %bitcast.8, s32[1,256]{1,0:T(1,128)} %bitcast.9, bf16[3,256,256]{2,1,0:T(8,128)(2,1)} %rest_3_.1, bf16[256,256]{1,0:T(8,128)(2,1)} %rest_4_.1, ...), custom_call_target="tpu_custom_call" | custom-call | tf_op jit(solution)/shard_map/pallas_call | solution.py:377
  41.6 11.0 %shard_map.104 = (bf16[128,256]{1,0:T(8,128)(2,1)}, f32[256,256]{1,0:T(8,128)}) custom-call(bf16[128,256]{1,0:T(8,128)(2,1)} %get-tuple-element.8.emb, f32[256,256]{1,0:T(8,128)} %get-tuple-element.9.grad), custom_call_target="tpu_custom_call" | custom-call | tf_op jit(solution)/shard_map/pallas_call | solution.py:433

commit v5 on v4

--- a/solution.py
+++ b/solution.py
@@ -351,15 +351,9 @@
         each(S - 1, lambda k: seg_copy(k, seg).wait_send())
 
 
-def hand_over(emb, grad, emb_out, grad_out, sems):
-    moves = [
-        pltpu.make_async_copy(emb, emb_out, sems.at[0]),
-        pltpu.make_async_copy(grad, grad_out, sems.at[1]),
-    ]
-    for move in moves:
-        move.start()
-    for move in moves:
-        move.wait()
+def hand_over(emb, grad, emb_out, grad_out):
+    emb_out[...] = emb[...]
+    grad_out[...] = grad[...]
 
 
 def on_device(S, Q, node_feats, adjacency, halo_rows, node_graph, layer_weights, bilinear, partners, ranking):
@@ -429,13 +423,11 @@
         partners.reshape(G * configs, partners.shape[2]),
         ranking,
     )
-    any_space = pl.BlockSpec(memory_space=pl.ANY)
     emb, grad = pl.pallas_call(
         hand_over,
         out_shape=(jax.ShapeDtypeStruct(emb.shape, bf16), jax.ShapeDtypeStruct(grad.shape, f32)),
-        in_specs=[any_space] * 2,
-        out_specs=(any_space, any_space),
-        scratch_shapes=[dma((2,))],
+        in_specs=[vmem] * 2,
+        out_specs=(vmem, vmem),
         compiler_params=pltpu.CompilerParams(vmem_limit_bytes=63 * 1024 * 1024),
     )(emb, grad)
     return emb.reshape(G, configs, feat), grad, loss.reshape(())

time: 54.6 us -> 45.2 us (0.83)
  Pallas kernels: 52 us -> 42.7 us
    pallas_call x1, Pallas kernels: 11 us -> 1.72 us  [on_device(): pl.pallas_call(hand_over, out_shape=(jax.ShapeDtypeStruct(emb.shape, bf16...]
where the time goes in v5:
time: 45.2 us; the launch traced here: 45.1 us
  Pallas kernels  42.7 us (94%)
  between operations  2.4 us (5%)
    pallas_call x1, Pallas kernels, on_device(): pl.pallas_call(functools.partial(kernel, sizes), out_shape=(jax.ShapeDtyp...  41 us
    pallas_call x1, Pallas kernels, on_device(): pl.pallas_call(hand_over, out_shape=(jax.ShapeDtypeStruct(emb.shape, bf16...  1.72 us

profile of v5, /device:TPU:0, one launch (start us, length us, event | category | flops | bytes accessed | tf_op | source)
XLA Modules:
  0.0 45.1 jit_solution(10669935709785030035)
XLA Ops:
  0.6 41.0 %shard_map.103 = (bf16[128,256]{1,0:T(8,128)(2,1)}, f32[256,256]{1,0:T(8,128)}, f32[1,1]{1,0:T(1,128)}) custom-call(bf16[32,256,256]{2,1,0:T(8,128)(2,1)} %feats.1, s32[288,256]{1,0:T(8,128)} %bitcast.6, s32[2,16]{1,0:T(2,128)} %bitcast.8, s32[1,256]{1,0:T(1,128)} %bitcast.9, bf16[3,256,256]{2,1,0:T(8,128)(2,1)} %rest_3_.1, bf16[256,256]{1,0:T(8,128)(2,1)} %rest_4_.1, ...), custom_call_target="tpu_custom_call" | custom-call | tf_op jit(solution)/shard_map/pallas_call | solution.py:371
  41.6 1.7 %shard_map.104 = (bf16[128,256]{1,0:T(8,128)(2,1)}, f32[256,256]{1,0:T(8,128)}) custom-call(bf16[128,256]{1,0:T(8,128)(2,1)} %get-tuple-element.8.emb, f32[256,256]{1,0:T(8,128)} %get-tuple-element.9.grad), custom_call_target="tpu_custom_call" | custom-call | tf_op jit(solution)/shard_map/pallas_call | solution.py:426

commit v6 on v5

--- a/solution.py
+++ b/solution.py
@@ -359,7 +359,7 @@
 def on_device(S, Q, node_feats, adjacency, halo_rows, node_graph, layer_weights, bilinear, partners, ranking):
     configs, nodes, feat = node_feats.shape
     rim, layers = halo_rows.shape[2], layer_weights.shape[0]
-    unroll = 8 if configs % 8 == 0 else 4
+    unroll = 16 if configs % 16 == 0 else 8 if configs % 8 == 0 else 4
     chunks = configs // unroll
     own_rows = max(16, G * configs // S)
     owners = G * configs // own_rows

time: 45.2 us -> 45.5 us (level)
  no operation moved by 1% of the time
where the time goes in v6:
time: 45.5 us; the launch traced here: 45.4 us
  Pallas kernels  43 us (95%)
  between operations  2.4 us (5%)
    pallas_call x1, Pallas kernels, on_device(): pl.pallas_call(functools.partial(kernel, sizes), out_shape=(jax.ShapeDtyp...  41.3 us
    pallas_call x1, Pallas kernels, on_device(): pl.pallas_call(hand_over, out_shape=(jax.ShapeDtypeStruct(emb.shape, bf16...  1.72 us

profile of v6, /device:TPU:0, one launch (start us, length us, event | category | flops | bytes accessed | tf_op | source)
XLA Modules:
  0.0 45.4 jit_solution(8681844319920476575)
XLA Ops:
  0.6 41.3 %shard_map.103 = (bf16[128,256]{1,0:T(8,128)(2,1)}, f32[256,256]{1,0:T(8,128)}, f32[1,1]{1,0:T(1,128)}) custom-call(bf16[32,256,256]{2,1,0:T(8,128)(2,1)} %feats.1, s32[288,256]{1,0:T(8,128)} %bitcast.6, s32[2,16]{1,0:T(2,128)} %bitcast.8, s32[1,256]{1,0:T(1,128)} %bitcast.9, bf16[3,256,256]{2,1,0:T(8,128)(2,1)} %rest_3_.1, bf16[256,256]{1,0:T(8,128)(2,1)} %rest_4_.1, ...), custom_call_target="tpu_custom_call" | custom-call | tf_op jit(solution)/shard_map/pallas_call | solution.py:371
  41.9 1.7 %shard_map.104 = (bf16[128,256]{1,0:T(8,128)(2,1)}, f32[256,256]{1,0:T(8,128)}) custom-call(bf16[128,256]{1,0:T(8,128)(2,1)} %get-tuple-element.8.emb, f32[256,256]{1,0:T(8,128)} %get-tuple-element.9.grad), custom_call_target="tpu_custom_call" | custom-call | tf_op jit(solution)/shard_map/pallas_call | solution.py:426
